TPU v7x, 512 devices: a whole 4x8x8 slice. The times are simulated.
512 devices in a mesh: inst: 16 (over x, y_hi), dom: 32 (over z, y_lo, core).
Axes of the slice: x: 4, y: 8 (y_hi: 4, y_lo: 2; y = y_hi * 2 + y_lo), z: 8, core: 2. Of those that a mesh axis runs over, the one named last changes fastest.
Arguments:
- flow_state: float32 [16, 5, 8192, 128], P('inst', None, 'dom'), may hold values from -6 to 6
- wave_speed: float32 [5], replicated, may hold values from 0.5 to 1.5
- frequency: float32 [1], replicated, may hold values from 0.05 to 0.3
- time_weights: float32 [16], replicated, may hold values from 0.05 to 0.5
- phase_shift: int32 [16], replicated, may hold values from 0 to 1023
- donor_part: int32 [1024, 4], replicated, may hold values from 0 to 31, as said below
- donor_block: int32 [1024, 4], replicated, may hold values from 0 to 255
- donor_count: int32 [1024], replicated, may hold values from 1 to 4
- donor_weight: float32 [1024, 4], replicated, may hold values from 0.1 to 1
Outputs:
- residual: float32 [16, 5, 8192, 128], P('inst', None, 'dom')
- interface_rows: float32 [16, 5, 1024, 128], P('inst', None, 'dom')
Inputs may be any that keep to these rules, and one draw needn't show every extreme that they name: `donor_part`: among the 128 entries of the rows of one partition, every partition appears exactly 4 times, padding entries included. Entries k >= donor_count[r] of row r are padding and carry no weight.
All inputs are finite; a program needn't handle non-finite values.
Results may differ from a plain program's by a relative error of at most 0.00007.
Values sent between devices are 32-bit elements; how exact they have to be, the bound alone decides.
A program may use at most 192 MiB of HBM per device.

v0:
```python
import jax
import jax.numpy as jnp
from jax import lax
from jax.sharding import PartitionSpec as P

highest = lax.Precision.HIGHEST


def extended(block, sides, width):
    for axis, dim in sides:
        count = lax.axis_size(axis)
        forward = [(i, i + 1) for i in range(count - 1)]
        backward = [(target, source) for source, target in forward]
        low = lax.ppermute(
            lax.slice_in_dim(block, block.shape[dim] - width, None, axis=dim), axis, forward
        )
        high = lax.ppermute(lax.slice_in_dim(block, 0, width, axis=dim), axis, backward)
        block = jnp.concatenate([low, block, high], axis=dim)
    return block


def time_table(length):
    indices = jnp.arange(length, dtype=jnp.int32)
    offset = indices[:, None] - indices[None, :]
    safe_off = jnp.where(offset == 0, 1, offset).astype(jnp.float32)
    signs = jnp.where(offset % 2 == 0, 1.0, -1.0).astype(jnp.float32)
    values_table = 0.5 * signs / jnp.tan(jnp.pi * safe_off / length)
    values_table = jnp.where(offset == 0, -2.0, values_table) + 2.0 / length
    return values_table


def body(
    flow_state,
    wave_speed,
    frequency,
    time_weights,
    phase_shift,
    donor_part,
    donor_block,
    donor_count,
    donor_weight,
):
    inst_count = lax.axis_size("inst")
    dom_count = lax.axis_size("dom")
    inst_index = lax.axis_index("inst")
    dom_index = lax.axis_index("dom")
    local_field = flow_state[0]
    spectral = time_table(inst_count)
    spectral_row = spectral[inst_index]
    columns = (jnp.arange(inst_count, dtype=jnp.int32) - phase_shift[inst_index]) % inst_count
    weight_row = time_weights[columns]
    factors = spectral_row
    derivative = jnp.einsum(
        "j,jvxz->vxz",
        factors,
        lax.all_gather(flow_state, "inst", axis=0, tiled=True),
        precision=highest,
    )
    padded = extended(local_field, (("dom", 1),), 1)
    upper_z = jnp.roll(local_field, -1, 2)
    lower_z = jnp.roll(local_field, 1, 2)
    laplace = padded[:, 2:] + padded[:, :-2] + upper_z + lower_z - 4.0 * local_field
    advect = wave_speed[:, None, None] * (upper_z - lower_z) * 0.5
    rows_dev = donor_part.shape[0] // dom_count
    donors = donor_part.shape[1]
    variables, cell_rows, pitch = local_field.shape
    own_part = lax.dynamic_slice_in_dim(donor_part, dom_index * rows_dev, rows_dev, 0)
    own_count = lax.dynamic_slice_in_dim(donor_count, dom_index * rows_dev, rows_dev, 0)
    own_weight = lax.dynamic_slice_in_dim(donor_weight, dom_index * rows_dev, rows_dev, 0)
    live_mask = (jnp.arange(donors, dtype=jnp.int32)[None, :] < own_count[:, None]).astype(
        jnp.float32
    )
    normed = own_weight * live_mask
    normed = normed / jnp.sum(normed, axis=1, keepdims=True)
    entries = rows_dev * donors
    capacity = entries // dom_count
    flat_part = donor_part.reshape(dom_count, entries)
    flat_block = donor_block.reshape(dom_count, entries)
    wanted = flat_part == dom_index
    ranking = jnp.cumsum(wanted.astype(jnp.int32), axis=1) - 1
    chosen = wanted[:, None, :] & (
        ranking[:, None, :] == jnp.arange(capacity, dtype=jnp.int32)[None, :, None]
    )
    send_rows = jnp.sum(jnp.where(chosen, flat_block[:, None, :], 0), axis=2)
    outgoing = local_field[:, send_rows.reshape(-1)]
    arrived = lax.all_to_all(outgoing, "dom", split_axis=1, concat_axis=1, tiled=True)
    own_flat = own_part.reshape(-1)
    positions = jnp.arange(entries, dtype=jnp.int32)
    matches = own_flat[:, None] == own_flat[None, :]
    earlier = positions[:, None] > positions[None, :]
    slot_index = jnp.sum(matches & earlier, axis=1)
    picked = arrived[:, own_flat * capacity + slot_index].reshape(
        variables, rows_dev, donors, pitch
    )
    mapped = jnp.einsum("vrkz,rk->vrz", picked, normed, precision=highest)
    factors = weight_row
    ghost_rows = jnp.einsum(
        "j,jvrz->vrz",
        factors,
        lax.all_gather(mapped[None], "inst", axis=0, tiled=True),
        precision=highest,
    )
    penalty = ghost_rows - local_field[:, :rows_dev]
    penalty = jnp.pad(penalty, ((0, 0), (0, cell_rows - rows_dev), (0, 0)))
    residual = 0.25 * laplace - advect - frequency[0] * derivative + 0.5 * penalty
    return (residual[None], ghost_rows[None])


def solution(mesh):
    in_specs = (P("inst", None, "dom", None), P(), P(), P(), P(), P(), P(), P(), P())
    out_specs = (P("inst", None, "dom", None), P("inst", None, "dom", None))
    return jax.shard_map(body, mesh=mesh, in_specs=in_specs, out_specs=out_specs, check_vma=False)
```

profile of v0, /device:TPU:1, one launch (start us, length us, event | category | flops | bytes accessed | tf_op | source)
XLA Modules:
  0.0 269.3 jit_solution(966662981916644038)
XLA Ops:
  7.2 0.7 broadcast_compare_fusion
  8.8 0.9 copy.29
  10.4 1.5 copy.55
  11.9 1.6 gather_fusion.1
  13.5 13.0 %all-to-all-start = ((f32[5,128,128]{2,0,1:T(8,128)}), f32[5,128,128]{2,0,1:T(8,128)S(1)}, u32[]{:S(2)}, u32[]{:S(2)}) async-start(f32[5,128,128]{2,0,1:T(8,128)} %bitcast.12), calls=%async_computation | async-start | bytes 1048576 | tf_op jit(solution)/shard_map/all_to_all | solution.py:86
  26.5 0.8 broadcast_multiply_fusion
  27.3 0.8 dynamic_slice.17
  28.2 0.8 fusion.23
  29.0 0.8 divide_bitcast_fusion
  30.3 12.9 %all-to-all-done = f32[5,128,128]{2,0,1:T(8,128)S(1)} async-done(((f32[5,128,128]{2,0,1:T(8,128)}), f32[5,128,128]{2,0,1:T(8,128)S(1)}, u32[]{:S(2)}, u32[]{:S(2)}) %all-to-all-start) | async-done | bytes 327712 | tf_op jit(solution)/shard_map/all_to_all | solution.py:86
  43.2 0.8 gather_fusion.2
  43.9 0.8 fusion.13
  45.4 0.7 all-gather.4.cloned.1.call-update
  46.1 3.5 %collective-permute-start = (f32[5,1,128]{2,0,1:T(8,128)S(1)}, f32[5,1,128]{2,0,1:T(8,128)S(1)}, u32[]{:S(2)}, u32[]{:S(2)}) collective-permute-start(f32[5,1,128]{2,0,1:T(8,128)S(1)} %get-tuple-element.14), channel_id=1, source_target_pairs={{1,0},{2,1},{3,2},{4,3},{5,4},{6,5},{7,6},{8,7},{9,8},{10,9},{11,1... | collective-permute-start | bytes 7688 | tf_op jit(solution)/shard_map/ppermute | solution.py:17
  49.6 3.2 %collective-permute-start.1 = (f32[5,1,128]{2,0,1:T(8,128)S(1)}, f32[5,1,128]{2,0,1:T(8,128)S(1)}, u32[]{:S(2)}, u32[]{:S(2)}) collective-permute-start(f32[5,1,128]{2,0,1:T(8,128)S(1)} %get-tuple-element.15), channel_id=1, source_target_pairs={{0,1},{1,2},{2,3},{3,4},{4,5},{5,6},{6,7},{7,8},{8,9},{9,10},{10,1... | collective-permute-start | bytes 7688 | tf_op jit(solution)/shard_map/ppermute | solution.py:14
  53.5 1.2 dynamic_slice.16
  55.4 0.7 gather_fusion
  56.4 1.8 fusion.48
  58.2 40.9 %all-gather.6.cloned.1.call-done = f32[80,32,128]{2,1,0:T(8,128)} async-done(((f32[5,32,128]{2,1,0:T(8,128)}), f32[80,32,128]{2,1,0:T(8,128)}) %all-gather.6.cloned.1.call-update) | async-done | bytes 1310736 | tf_op jit(solution)/shard_map/all_gather | solution.py:100
  99.2 2.7 %fusion.2 = f32[1,5,32,128]{3,0,2,1:T(1,128)S(1)} fusion(f32[16,5,32,128]{3,2,1,0:T(8,128)} %bitcast.56, f32[16]{0:T(128)S(1)} %gather_fusion), kind=kOutput, calls=%fused_computation.5 | convolution fusion | flops 3932160 | bytes 1392704 | tf_op jit(solution)/shard_map/j,jvrz->vrz/dot_general | solution.py:97
  102.0 142.9 %all-gather.4.cloned.1.call-done = f32[16,5,256,128]{3,2,1,0:T(8,128)} async-done(((f32[1,5,256,128]{3,2,1,0:T(8,128)}), f32[16,5,256,128]{3,2,1,0:T(8,128)}) %all-gather.4.cloned.1.call-update) | async-done | bytes 10485776 | tf_op jit(solution)/shard_map/all_gather | solution.py:56
  244.8 15.5 %fusion = f32[1,5,256,128]{3,0,2,1:T(1,128)S(1)} fusion(f32[16,5,256,128]{3,2,1,0:T(8,128)} %all-gather.4.cloned.1.call-done, pred[16,16]{1,0:T(8,128)(4,1)S(1)} %fusion.19, s32[]{:T(128)S(6)} %select_n.79, s32[16,16]{1,0:T(8,128)S(1)} %get-tuple-element.17, s32[16,16]{1,0:T(8,128)S(1)} %get-tuple-element.16), kind=kOutput, calls=%fused_computation.3 | convolution fusion | flops 31457408 | bytes 11142660 | tf_op jit(solution)/shard_map/j,jvxz->vxz/dot_general | solution.py:53
  260.4 1.1 fusion.12
  261.5 1.0 copy.33
  (42 shorter events, 4.1 us)
Async XLA Ops:
  7.2 48.2 %copy-start = (f32[16]{0:T(128)S(1)}, f32[16]{0:T(128)}, u32[]{:S(2)}) copy-start(f32[16]{0:T(128)} %param.12) | copy-start | bytes 196
  13.5 29.7 %all-to-all-start = ((f32[5,128,128]{2,0,1:T(8,128)}), f32[5,128,128]{2,0,1:T(8,128)S(1)}, u32[]{:S(2)}, u32[]{:S(2)}) async-start(f32[5,128,128]{2,0,1:T(8,128)} %bitcast.12), calls=%async_computation | async-start | bytes 1048576 | tf_op jit(solution)/shard_map/all_to_all | solution.py:86
  26.5 72.7 %all-gather.6.cloned.1.call-start = ((), (), s32[]{:S(2)}) async-start(), calls=%async_computation.2 | async-start | bytes 1392640 | tf_op jit(solution)/shard_map/all_gather | solution.py:100
  45.4 199.5 %all-gather.4.cloned.1.call-start = ((), (), s32[]{:S(2)}) async-start(), calls=%async_computation.1 | async-start | bytes 11141120 | tf_op jit(solution)/shard_map/all_gather | solution.py:56
  46.1 214.2 %collective-permute-start = (f32[5,1,128]{2,0,1:T(8,128)S(1)}, f32[5,1,128]{2,0,1:T(8,128)S(1)}, u32[]{:S(2)}, u32[]{:S(2)}) collective-permute-start(f32[5,1,128]{2,0,1:T(8,128)S(1)} %get-tuple-element.14), channel_id=1, source_target_pairs={{1,0},{2,1},{3,2},{4,3},{5,4},{6,5},{7,6},{8,7},{9,8},{10,9},{11,1... | collective-permute-start | bytes 7688 | tf_op jit(solution)/shard_map/ppermute | solution.py:17
  49.6 210.7 %collective-permute-start.1 = (f32[5,1,128]{2,0,1:T(8,128)S(1)}, f32[5,1,128]{2,0,1:T(8,128)S(1)}, u32[]{:S(2)}, u32[]{:S(2)}) collective-permute-start(f32[5,1,128]{2,0,1:T(8,128)S(1)} %get-tuple-element.15), channel_id=1, source_target_pairs={{0,1},{1,2},{2,3},{3,4},{4,5},{5,6},{6,7},{7,8},{8,9},{9,10},{10,1... | collective-permute-start | bytes 7688 | tf_op jit(solution)/shard_map/ppermute | solution.py:14
  56.1 204.3 %copy-start.4 = (f32[5]{0:T(128)S(1)}, f32[5]{0:T(128)}, u32[]{:S(2)}) copy-start(f32[5]{0:T(128)} %param.10) | copy-start | bytes 64
  101.9 160.5 %copy-start.3 = (f32[1,5,32,128]{3,0,2,1:T(1,128)}, f32[1,5,32,128]{3,0,2,1:T(1,128)S(1)}, u32[]{:S(2)}) copy-start(f32[1,5,32,128]{3,0,2,1:T(1,128)S(1)} %fusion.2) | copy-start | bytes 245764
  244.8 15.6 %copy-start.1 = (f32[5,256,127]{2,0,1:T(8,128)S(1)}, f32[5,256,127]{2,0,1:T(8,128)}, u32[]{:S(2)}) copy-start(f32[5,256,127]{2,0,1:T(8,128)} %get-tuple-element.10) | copy-start | bytes 1950724
  244.8 15.6 %copy-start.2 = (f32[5,256,127]{2,0,1:T(8,128)S(1)}, f32[5,256,127]{2,0,1:T(8,128)}, u32[]{:S(2)}) copy-start(f32[5,256,127]{2,0,1:T(8,128)} %get-tuple-element.11) | copy-start | bytes 1950724
Sparse Core Ops, SparseCore 0:
  45.5 53.6 all-gather.5
  102.2 142.5 all-gather.3
where the time goes:
time: 270 us; the launch traced here: 269 us
  waiting for transfers between devices  197 us (73%)
  starting transfers between devices  19.7 us (7%)
  matrix products  19 us (7%)
  between operations  14.9 us (6%)
  local copies, waits for them, and re-layouts  12.7 us (5%)
  other arithmetic  5.46 us (2%)
    all_gather x1, waiting for transfers between devices, body(): lax.all_gather(flow_state, 'inst', axis=0, tiled=True)  143 us
    all_gather x1, waiting for transfers between devices, body(): lax.all_gather(mapped[None], 'inst', axis=0, tiled=True)  40.9 us
    dot_general x1, matrix products, body(): jnp.einsum('j,jvxz->vxz', factors, lax.all_gather(flow_state, 'inst', axi...  15.5 us
    all_to_all x1, starting transfers between devices, body(): lax.all_to_all(outgoing, 'dom', split_axis=1, concat_axis=1, tiled=True)  13 us
    all_to_all x1, waiting for transfers between devices, body(): lax.all_to_all(outgoing, 'dom', split_axis=1, concat_axis=1, tiled=True)  12.9 us
  transfers between devices with their start and end apart: 5, of which 3 were waited for; matrix products, arithmetic and copies ran while one was open for 10% of the time, Pallas kernels for 0%

commit v1 on v0

v1 whole, which is shorter than its diff:
```python
import functools

import jax
import jax.numpy as jnp
import numpy as np
from jax import lax
from jax.experimental import pallas as pl
from jax.experimental.pallas import tpu as pltpu
from jax.sharding import PartitionSpec as P

HIGHEST = lax.Precision.HIGHEST
MESH = pl.DeviceIdType.MESH
GROUPS = ((0, 2), (2, 4), (4, 5))


def spectral_line(length):
    j = np.arange(length)
    safe = np.where(j == 0, 1, j)
    line = 0.5 * np.where(j % 2 == 0, 1.0, -1.0) / np.tan(np.pi * safe / length)
    return np.where(j == 0, -2.0, line) + 2.0 / length


def iota(shape, dim):
    return lax.broadcasted_iota(jnp.int32, shape, dim)


def send_table(part_ref, block_ref, dom, ndom, rows, donors):
    lanes = 128
    chunks = ndom * rows // lanes
    parts = jnp.concatenate([part_ref[:, lanes * g : lanes * (g + 1)] for g in range(chunks)], axis=0)
    blocks = jnp.concatenate([block_ref[:, lanes * g : lanes * (g + 1)] for g in range(chunks)], axis=0)
    count = chunks * donors
    cap = rows * donors // ndom
    per = lanes // rows
    wanted = parts == dom
    ones = jnp.where(wanted, 1.0, 0.0)
    a, b = iota((lanes, lanes), 0), iota((lanes, lanes), 1)
    same = (a // rows) == (b // rows)
    before = jnp.where(same & (a < b), 1.0, 0.0)
    whole = jnp.where(same, 1.0, 0.0)
    ra, rb = iota((count, count), 0), iota((count, count), 1)
    lower = jnp.where(((ra // donors) == (rb // donors)) & (rb < ra), 1.0, 0.0)
    dot = functools.partial(jnp.dot, preferred_element_type=jnp.float32)
    rank = dot(ones, before) + dot(lower, dot(ones, whole))
    total = jnp.zeros((count, lanes), jnp.float32)
    values = blocks.astype(jnp.float32)
    for c in range(cap):
        picked = jnp.where(wanted & (rank == float(c)), values, 0.0)
        spread = jnp.where((b % (per * cap)) == (a // rows) * cap + c, 1.0, 0.0)
        total = total + dot(picked, spread)
    row, lane = iota((count, lanes), 0), iota((count, lanes), 1)
    line = jnp.sum(
        jnp.where((lane // (per * cap)) == (row // donors), total, 0.0), axis=0, keepdims=True
    )
    return jnp.transpose(jnp.broadcast_to(line, (lanes, lanes)))


def weight_table(part_ref, weight_ref, count_ref, dom, ndom, rows, donors):
    lanes = 128
    per = lanes // rows
    cap = rows * donors // ndom
    at = pl.ds(pl.multiple_of((dom // per) * lanes, lanes), lanes)
    own = jnp.concatenate(
        [
            part_ref[:, at].astype(jnp.float32),
            weight_ref[:, at],
            jnp.broadcast_to(count_ref[:, at].astype(jnp.float32), (8, lanes)),
        ],
        axis=0,
    )
    a, b = iota((lanes, lanes), 0), iota((lanes, lanes), 1)
    pick = jnp.where(a == (dom % per) * rows + b % rows, 1.0, 0.0)
    own = jnp.dot(own, pick, precision=HIGHEST, preferred_element_type=jnp.float32)
    row, lane = iota((donors, lanes), 0), iota((donors, lanes), 1)
    mine = (lane // rows) == row
    part = jnp.sum(jnp.where(mine, own[:donors], 0.0), axis=0, keepdims=True)
    live = mine & (row.astype(jnp.float32) < own[2 * donors : 3 * donors])
    weight = jnp.sum(jnp.where(live, own[donors : 2 * donors], 0.0), axis=0, keepdims=True)
    part_row = jnp.broadcast_to(part, (lanes, lanes))
    part_col = jnp.transpose(part_row)
    rank = jnp.sum(jnp.where((part_row == part_col) & (a < b), 1.0, 0.0), axis=0, keepdims=True)
    slot_col = jnp.transpose(jnp.broadcast_to(part * cap + rank, (lanes, lanes)))
    weight_col = jnp.transpose(jnp.broadcast_to(weight, (lanes, lanes)))
    spread = jnp.where(slot_col == b.astype(jnp.float32), weight_col, 0.0)
    top = sum(spread[rows * k : rows * (k + 1)] for k in range(donors))
    bottom = sum(weight_col[rows * k : rows * (k + 1)] for k in range(donors))
    return top / bottom


def kernel(
    ninst,
    ndom,
    x,
    speed,
    freq,
    time_weights,
    shift,
    part,
    block,
    weight,
    count,
    res,
    ghost,
    sbuf,
    rbuf,
    fbuf,
    obuf,
    back,
    mbuf,
    mrec,
    gout,
    gback,
    hsend,
    hrecv,
    wtab,
    d_send,
    d_recv,
    f_send,
    f_recv,
    b_send,
    b_recv,
    m_send,
    m_recv,
    g_send,
    g_recv,
    h_send,
    h_recv,
):
    nv, cells, pitch = x.shape
    rows = ghost.shape[1]
    donors = part.shape[0]
    cap = rows * donors // ndom
    cut = cells // ninst
    fine = rows // ninst
    me, dom = lax.axis_index("inst"), lax.axis_index("dom")

    def inst_of(k):
        return lax.rem(me + k, ninst)

    def dom_of(k):
        return lax.rem(dom + k, ndom)

    def own_rows(i):
        return pl.ds(pl.multiple_of(i * cut, cut), cut)

    def remote(src, dst, send, recv, to):
        return pltpu.make_async_remote_copy(
            src_ref=src, dst_ref=dst, send_sem=send, recv_sem=recv, device_id=to, device_id_type=MESH
        )

    def donor_copy(k):
        to = dom_of(k)
        return remote(sbuf.at[to], rbuf.at[dom], d_send.at[k], d_recv.at[ndom - k], (me, to))

    def donor_arrival(k):
        return remote(sbuf.at[0], rbuf.at[dom_of(k)], d_send.at[k], d_recv.at[k], (me, dom_of(k)))

    def forward_copy(g, k):
        v0, v1 = GROUPS[g]
        to = inst_of(k)
        return remote(
            x.at[v0:v1, own_rows(to)],
            fbuf.at[ninst - k, v0:v1],
            f_send.at[g, k],
            f_recv.at[g, ninst - k],
            (to, dom),
        )

    def forward_arrival(g, k):
        v0, v1 = GROUPS[g]
        return remote(
            x.at[v0:v1, own_rows(me)], fbuf.at[k, v0:v1], f_send.at[g, k], f_recv.at[g, k], (inst_of(k), dom)
        )

    def back_copy(g, k):
        v0, v1 = GROUPS[g]
        return remote(
            obuf.at[k, v0:v1],
            back.at[v0:v1, own_rows(me)],
            b_send.at[g, k],
            b_recv.at[g, ninst - k],
            (inst_of(k), dom),
        )

    def back_arrival(g, k):
        v0, v1 = GROUPS[g]
        return remote(
            obuf.at[k, v0:v1], back.at[v0:v1, own_rows(inst_of(k))], b_send.at[g, k], b_recv.at[g, k], (inst_of(k), dom)
        )

    def mapped_copy(k):
        to = inst_of(k)
        return remote(mbuf.at[to], mrec.at[ninst - k], m_send.at[k], m_recv.at[ninst - k], (to, dom))

    def mapped_arrival(k):
        return remote(mbuf.at[0], mrec.at[k], m_send.at[k], m_recv.at[k], (inst_of(k), dom))

    def ghost_copy(k):
        return remote(gout.at[k], gback.at[me], g_send.at[k], g_recv.at[ninst - k], (inst_of(k), dom))

    def ghost_arrival(k):
        return remote(gout.at[k], gback.at[inst_of(k)], g_send.at[k], g_recv.at[k], (inst_of(k), dom))

    def halo_copy(side):
        to = dom_of(1 if side == 0 else ndom - 1)
        return remote(hsend.at[side], hrecv.at[side], h_send.at[side], h_recv.at[side], (me, to))

    def each(count, act):
        def step(k, carry):
            act(k)
            return carry

        lax.fori_loop(1, count, step, 0)

    barrier = pltpu.get_barrier_semaphore()
    each(ndom, lambda k: pl.semaphore_signal(barrier, inc=1, device_id=(me, dom_of(k)), device_id_type=MESH))
    each(ninst, lambda k: pl.semaphore_signal(barrier, inc=1, device_id=(inst_of(k), dom), device_id_type=MESH))

    column = send_table(part, block, dom, ndom, rows, donors)
    lane = iota(column.shape, 1).astype(jnp.float32)
    chosen = jnp.concatenate(
        [jnp.where(column == lane + float(s), 1.0, 0.0) for s in range(0, cells, 128)], axis=1
    )
    for v in range(nv):
        out = jnp.dot(chosen, x[v], precision=HIGHEST, preferred_element_type=jnp.float32)
        for q in range(ndom):
            sbuf[q, v] = out[q * cap : (q + 1) * cap]
        hsend[0, v] = x[v, cells - 1 :, :]
        hsend[1, v] = x[v, :1, :]

    pl.semaphore_wait(barrier, ndom - 1 + ninst - 1)
    halo_copy(0).start()
    halo_copy(1).start()
    each(ndom, lambda k: donor_copy(k).start())
    for g in range(len(GROUPS)):
        each(ninst, lambda k: forward_copy(g, k).start())

    rbuf[dom] = sbuf[dom]
    for v in range(nv):
        fbuf[0, v] = x[v, own_rows(me), :]

    def weights_of(target, carry):
        phase = shift[inst_of(target)]
        for k in range(ninst):
            wtab[target * ninst + k] = time_weights[jnp.bitwise_and(me + k - phase, ninst - 1)]
        return carry

    lax.fori_loop(0, ninst, weights_of, 0)
    table = weight_table(part, weight, count, dom, ndom, rows, donors)

    halo_copy(0).wait_recv()
    halo_copy(1).wait_recv()
    edge = iota((cells, pitch), 0)
    for v in range(nv):
        u = x[v]
        low = jnp.where(dom == 0, 0.0, hrecv[0, v])
        high = jnp.where(dom == ndom - 1, 0.0, hrecv[1, v])
        below = jnp.where(edge == 0, low, pltpu.roll(u, 1, 0))
        above = jnp.where(edge == cells - 1, high, pltpu.roll(u, cells - 1, 0))
        upper = pltpu.roll(u, pitch - 1, 1)
        lower = pltpu.roll(u, 1, 1)
        base = 0.25 * (above + below + upper + lower - 4.0 * u) - speed[v] * (upper - lower) * 0.5
        res[v] = base
        res[v, :rows] = base[:rows] - 0.5 * u[:rows]

    line = spectral_line(ninst)
    half = ninst // 2
    even = [float(np.float32(0.5 * (line[j] + line[j + half]))) for j in range(half)]
    odd = [float(np.float32(0.5 * (line[j] - line[j + half]))) for j in range(half)]
    scale = -freq[0]

    def mix(g):
        v0, v1 = GROUPS[g]
        each(ninst, lambda k: forward_arrival(g, k).wait_recv())

        def tile(t, carry):
            v = v0 + t // (cut // 8)
            r = pl.multiple_of((t % (cut // 8)) * 8, 8)
            f = [fbuf[k, v, pl.ds(r, 8), :] for k in range(ninst)]
            e = [scale * (f[k] + f[k + half]) for k in range(half)]
            o = [scale * (f[k] - f[k + half]) for k in range(half)]
            for target in range(half):
                total_e = total_o = None
                for k in range(half):
                    j = target - k
                    ce = even[j % half]
                    co = odd[j] if j >= 0 else -odd[j + half]
                    total_e = ce * e[k] if total_e is None else total_e + ce * e[k]
                    total_o = co * o[k] if total_o is None else total_o + co * o[k]
                if target == 0:
                    back[v, pl.ds(pl.multiple_of(me * cut + r, 8), 8), :] = total_e + total_o
                else:
                    obuf[target, v, pl.ds(r, 8), :] = total_e + total_o
                obuf[target + half, v, pl.ds(r, 8), :] = total_e - total_o
            return carry

        lax.fori_loop(0, (v1 - v0) * (cut // 8), tile, 0)
        each(ninst, lambda k: back_copy(g, k).start())

    def remap():
        each(ndom, lambda k: donor_arrival(k).wait_recv())
        for v in range(nv):
            arrived = jnp.concatenate([rbuf[p, v] for p in range(ndom)], axis=0)
            rows_v = jnp.dot(table, arrived, precision=HIGHEST, preferred_element_type=jnp.float32)
            for s in range(ninst):
                mbuf[s, fine * v : fine * (v + 1)] = rows_v[fine * s : fine * (s + 1)]
        each(ninst, lambda k: mapped_copy(k).start())
        mrec[0] = mbuf[me]

    def interpolate():
        each(ninst, lambda k: mapped_arrival(k).wait_recv())

        def one(target, carry):
            total = wtab[target * ninst] * mrec[0]
            for k in range(1, ninst):
                total = total + wtab[target * ninst + k] * mrec[k]
            gout[target] = total
            return carry

        lax.fori_loop(0, ninst, one, 0)
        each(ninst, lambda k: ghost_copy(k).start())
        gback[me] = gout[0]

    remap()
    mix(0)
    mix(1)
    interpolate()
    mix(2)

    for g, (v0, v1) in enumerate(GROUPS):
        each(ninst, lambda k: back_arrival(g, k).wait_recv())
        for v in range(v0, v1):
            res[v] = res[v] + back[v]
    each(ninst, lambda k: ghost_arrival(k).wait_recv())
    for v in range(nv):
        full = jnp.concatenate([gback[s, fine * v : fine * (v + 1)] for s in range(ninst)], axis=0)
        ghost[v] = full
        res[v, :rows] = res[v, :rows] + 0.5 * full

    halo_copy(0).wait_send()
    halo_copy(1).wait_send()
    each(ndom, lambda k: donor_copy(k).wait_send())
    for g in range(len(GROUPS)):
        each(ninst, lambda k: forward_copy(g, k).wait_send())
        each(ninst, lambda k: back_copy(g, k).wait_send())
    each(ninst, lambda k: mapped_copy(k).wait_send())
    each(ninst, lambda k: ghost_copy(k).wait_send())


def solution(mesh):
    ninst, ndom = mesh.shape["inst"], mesh.shape["dom"]

    def body(flow_state, speed, freq, time_weights, shift, part, block, count, weight):
        x = flow_state[0]
        nv, cells, pitch = x.shape
        rows = part.shape[0] // ndom
        donors = part.shape[1]
        cap = rows * donors // ndom
        cut = cells // ninst
        fine = rows // ninst
        groups = len(GROUPS)
        vmem = pl.BlockSpec(memory_space=pltpu.VMEM)
        smem = pl.BlockSpec(memory_space=pltpu.SMEM)
        f32 = jnp.float32
        dma = pltpu.SemaphoreType.DMA
        res, ghost = pl.pallas_call(
            functools.partial(kernel, ninst, ndom),
            out_shape=(
                jax.ShapeDtypeStruct((nv, cells, pitch), f32),
                jax.ShapeDtypeStruct((nv, rows, pitch), f32),
            ),
            in_specs=[vmem, smem, smem, smem, smem, vmem, vmem, vmem, vmem],
            out_specs=(vmem, vmem),
            scratch_shapes=[
                pltpu.VMEM((ndom, nv, cap, pitch), f32),
                pltpu.VMEM((ndom, nv, cap, pitch), f32),
                pltpu.VMEM((ninst, nv, cut, pitch), f32),
                pltpu.VMEM((ninst, nv, cut, pitch), f32),
                pltpu.VMEM((nv, cells, pitch), f32),
                pltpu.VMEM((ninst, nv * fine, pitch), f32),
                pltpu.VMEM((ninst, nv * fine, pitch), f32),
                pltpu.VMEM((ninst, nv * fine, pitch), f32),
                pltpu.VMEM((ninst, nv * fine, pitch), f32),
                pltpu.VMEM((2, nv, 1, pitch), f32),
                pltpu.VMEM((2, nv, 1, pitch), f32),
                pltpu.SMEM((ninst * ninst,), f32),
                dma((ndom,)),
                dma((ndom,)),
                dma((groups, ninst)),
                dma((groups, ninst)),
                dma((groups, ninst)),
                dma((groups, ninst)),
                dma((ninst,)),
                dma((ninst,)),
                dma((ninst,)),
                dma((ninst,)),
                dma((2,)),
                dma((2,)),
            ],
            compiler_params=pltpu.CompilerParams(
                collective_id=0, has_side_effects=True, vmem_limit_bytes=40 << 20
            ),
            name="harmonic_residual",
        )(x, speed, freq, time_weights, shift, part.T, block.T, weight.T, count[None])
        return res[None], ghost[None]

    in_specs = (P("inst", None, "dom", None), P(), P(), P(), P(), P(), P(), P(), P())
    out_specs = (P("inst", None, "dom", None), P("inst", None, "dom", None))
    return jax.shard_map(body, mesh=mesh, in_specs=in_specs, out_specs=out_specs, check_vma=False)
```

time: 270 us -> 65.8 us (0.24)
  waiting for transfers between devices: 197 us -> 0 us
  Pallas kernels: 0 us -> 58.7 us
  starting transfers between devices: 19.7 us -> 0 us
  matrix products: 19 us -> 0 us
  between operations: 14.9 us -> 1.32 us
  local copies, waits for them, and re-layouts: 12.7 us -> 5.38 us
  other arithmetic: 5.46 us -> 0 us
    all_gather x2 -> x0, waiting for transfers between devices: 184 us -> none  [the longest x1 143 us: body(): lax.all_gather(flow_state, 'inst', axis=0, tiled=True)]
    pallas_call x0 -> x1, Pallas kernels: none -> 58.7 us  [body(): pl.pallas_call(functools.partial(kernel, ninst, ndom), out_shape=(jax.Sha...]
    dot_general x3 -> x0, matrix products: 19 us -> none  [the longest x1 15.5 us: body(): jnp.einsum('j,jvxz->vxz', factors, lax.all_gather(flow_state, 'inst', axi...]
    all_to_all x1 -> x0, starting transfers between devices: 13 us -> none  [body(): lax.all_to_all(outgoing, 'dom', split_axis=1, concat_axis=1, tiled=True)]
    all_to_all x1 -> x0, waiting for transfers between devices: 12.9 us -> none  [body(): lax.all_to_all(outgoing, 'dom', split_axis=1, concat_axis=1, tiled=True)]
    ppermute x2 -> x0, starting transfers between devices: 6.67 us -> none  [the longest x1 3.5 us: extended(): lax.ppermute(lax.slice_in_dim(block, 0, width, axis=dim), axis, backward)]
    gather x3 -> x0, local copies, waits for them, and re-layouts: 2.97 us -> none  [the longest x1 1.55 us: body(): outgoing = local_field[:, send_rows.reshape(-1)]]
  transfers between devices with their start and end apart: 5 -> 0, of which waited for: 3 -> 0; matrix products, arithmetic and copies ran while one was open for 10% -> 0% of each run, Pallas kernels for 0% -> 0%
where the time goes in v1:
time: 65.8 us; the launch traced here: 65.4 us
  Pallas kernels  58.7 us (89%)
  local copies, waits for them, and re-layouts  5.38 us (8%)
  between operations  1.32 us (2%)
    pallas_call x1, Pallas kernels, body(): pl.pallas_call(functools.partial(kernel, ninst, ndom), out_shape=(jax.Sha...  58.7 us
    unnamed x18, local copies, waits for them, and re-layouts  5.38 us

profile of v1, /device:TPU:1, one launch (start us, length us, event | category | flops | bytes accessed | tf_op | source)
XLA Modules:
  0.0 65.4 jit_solution(13490938060151202679)
XLA Ops:
  1.3 0.0 copy-start.4
  1.3 0.0 copy-start.5
  1.3 0.0 copy-start.6
  1.3 0.0 copy-start.7
  1.3 0.6 copy-done.4
  2.0 0.0 copy-done.5
  2.0 0.0 copy-done.6
  2.0 0.0 copy-done.7
  2.0 0.0 copy-start
  2.0 1.1 %copy-done = f32[1,5,256,128]{3,2,1,0:T(8,128)S(1)} copy-done((f32[1,5,256,128]{3,2,1,0:T(8,128)S(1)}, f32[1,5,256,128]{3,2,1,0:T(8,128)}, u32[]{:S(2)}) %copy-start) | copy-done | bytes 655384
  3.1 0.0 copy-start.1
  3.1 0.7 %copy-done.1 = s32[1024,4]{0,1:T(4,128)S(1)} copy-done((s32[1024,4]{0,1:T(4,128)S(1)}, s32[1024,4]{0,1:T(4,128)}, u32[]{:S(2)}) %copy-start.1) | copy-done | bytes 16408
  3.8 0.0 copy-start.2
  3.8 0.7 %copy-done.2 = s32[1024,4]{0,1:T(4,128)S(1)} copy-done((s32[1024,4]{0,1:T(4,128)S(1)}, s32[1024,4]{0,1:T(4,128)}, u32[]{:S(2)}) %copy-start.2) | copy-done | bytes 16408
  4.5 0.0 copy-start.3
  4.5 0.7 %copy-done.3 = f32[1024,4]{0,1:T(4,128)S(1)} copy-done((f32[1024,4]{0,1:T(4,128)S(1)}, f32[1024,4]{0,1:T(4,128)}, u32[]{:S(2)}) %copy-start.3) | copy-done | bytes 16408
  5.2 58.7 %harmonic_residual.1 = (f32[5,256,128]{2,1,0:T(8,128)S(1)}, f32[5,32,128]{2,1,0:T(8,128)S(1)}) custom-call(f32[5,256,128]{2,1,0:T(8,128)S(1)} %bitcast.7, f32[5]{0:T(128)S(1)} %copy-done.5, f32[1]{0:T(128)S(6)} %copy.13.freq, f32[16]{0:T(128)S(1)} %copy-done.6, s32[16]{0:T(128)S(1)} %copy-done.7, s32[4,1024]{1,0:T(4,128)S(1)} %bitcast.10, ...), custom_call_target="tpu_custom_call" | custom-call | tf_op jit(solution)/shard_map/harmonic_residual/pallas_call | solution.py:366
  63.9 0.8 %copy.14 = f32[1,5,256,128]{3,2,1,0:T(8,128)} copy(f32[1,5,256,128]{3,2,1,0:T(8,128)S(1)} %bitcast.8) | data formatting | bytes 1310720
  64.7 0.6 copy.15
Async XLA Ops:
  1.3 0.7 %copy-start.4 = (s32[1024]{0:T(1024)S(1)}, s32[1024]{0:T(1024)}, u32[]{:S(2)}) copy-start(s32[1024]{0:T(1024)} %param.16) | copy-start | bytes 12292
  1.3 0.7 %copy-start.5 = (f32[5]{0:T(128)S(1)}, f32[5]{0:T(128)}, u32[]{:S(2)}) copy-start(f32[5]{0:T(128)} %speed.1) | copy-start | bytes 64
  1.3 0.7 %copy-start.6 = (f32[16]{0:T(128)S(1)}, f32[16]{0:T(128)}, u32[]{:S(2)}) copy-start(f32[16]{0:T(128)} %time_weights.1) | copy-start | bytes 196
  1.3 0.7 %copy-start.7 = (s32[16]{0:T(128)S(1)}, s32[16]{0:T(128)}, u32[]{:S(2)}) copy-start(s32[16]{0:T(128)} %shift.1) | copy-start | bytes 196
  2.0 1.1 %copy-start = (f32[1,5,256,128]{3,2,1,0:T(8,128)S(1)}, f32[1,5,256,128]{3,2,1,0:T(8,128)}, u32[]{:S(2)}) copy-start(f32[1,5,256,128]{3,2,1,0:T(8,128)} %param.9) | copy-start | bytes 1966084
  3.1 0.7 %copy-start.1 = (s32[1024,4]{0,1:T(4,128)S(1)}, s32[1024,4]{0,1:T(4,128)}, u32[]{:S(2)}) copy-start(s32[1024,4]{0,1:T(4,128)} %param.14) | copy-start | bytes 49156
  3.8 0.7 %copy-start.2 = (s32[1024,4]{0,1:T(4,128)S(1)}, s32[1024,4]{0,1:T(4,128)}, u32[]{:S(2)}) copy-start(s32[1024,4]{0,1:T(4,128)} %param.15) | copy-start | bytes 49156
  4.5 0.7 %copy-start.3 = (f32[1024,4]{0,1:T(4,128)S(1)}, f32[1024,4]{0,1:T(4,128)}, u32[]{:S(2)}) copy-start(f32[1024,4]{0,1:T(4,128)} %param.17) | copy-start | bytes 49156

commit v2 on v1

--- a/solution.py
+++ b/solution.py
@@ -9,8 +9,10 @@
 from jax.sharding import PartitionSpec as P
 
 HIGHEST = lax.Precision.HIGHEST
+VMEM = 56 << 20
 MESH = pl.DeviceIdType.MESH
 GROUPS = ((0, 2), (2, 4), (4, 5))
+ORDER = (2, 10, 6, 14, 9, 5, 11, 7, 1, 13, 3, 15, 8, 4, 12)
 
 
 def spectral_line(length):
@@ -46,7 +48,8 @@
     values = blocks.astype(jnp.float32)
     for c in range(cap):
         picked = jnp.where(wanted & (rank == float(c)), values, 0.0)
-        spread = jnp.where((b % (per * cap)) == (a // rows) * cap + c, 1.0, 0.0)
+        group = a // rows
+        spread = jnp.where((b % (per * cap)) == ((group % 2) * 2 + group // 2) * cap + c, 1.0, 0.0)
         total = total + dot(picked, spread)
     row, lane = iota((count, lanes), 0), iota((count, lanes), 1)
     line = jnp.sum(
@@ -55,7 +58,7 @@
     return jnp.transpose(jnp.broadcast_to(line, (lanes, lanes)))
 
 
-def weight_table(part_ref, weight_ref, count_ref, dom, ndom, rows, donors):
+def weight_table(part_ref, weight_ref, count_ref, dom, side, ndom, rows, donors):
     lanes = 128
     per = lanes // rows
     cap = rows * donors // ndom
@@ -79,7 +82,11 @@
     part_row = jnp.broadcast_to(part, (lanes, lanes))
     part_col = jnp.transpose(part_row)
     rank = jnp.sum(jnp.where((part_row == part_col) & (a < b), 1.0, 0.0), axis=0, keepdims=True)
-    slot_col = jnp.transpose(jnp.broadcast_to(part * cap + rank, (lanes, lanes)))
+    named = part.astype(jnp.int32)
+    site = (named // 4) * 2 + named % 2
+    slot = (site * 2 + (dom // 2) % 2).astype(jnp.float32) * cap + rank
+    slot = jnp.where((named // 2) % 2 == side, slot, -1.0)
+    slot_col = jnp.transpose(jnp.broadcast_to(slot, (lanes, lanes)))
     weight_col = jnp.transpose(jnp.broadcast_to(weight, (lanes, lanes)))
     spread = jnp.where(slot_col == b.astype(jnp.float32), weight_col, 0.0)
     top = sum(spread[rows * k : rows * (k + 1)] for k in range(donors))
@@ -90,6 +97,17 @@
 def kernel(
     ninst,
     ndom,
+    x_in,
+    speed_in,
+    freq_in,
+    time_weights_in,
+    shift_in,
+    part_in,
+    block_in,
+    weight_in,
+    count_in,
+    res_out,
+    ghost_out,
     x,
     speed,
     freq,
@@ -99,13 +117,17 @@
     block,
     weight,
     count,
+    loads,
     res,
     ghost,
+    stores,
     sbuf,
     rbuf,
     fbuf,
     obuf,
     back,
+    psend,
+    precv,
     mbuf,
     mrec,
     gout,
@@ -119,6 +141,8 @@
     f_recv,
     b_send,
     b_recv,
+    p_send,
+    p_recv,
     m_send,
     m_recv,
     g_send,
@@ -140,6 +164,17 @@
     def dom_of(k):
         return lax.rem(dom + k, ndom)
 
+    nsite = ndom // 2
+    side = (dom // 2) % 2
+    site = (dom // 4) * 2 + dom % 2
+    mate = dom + 2 - 4 * side
+
+    def site_of(k):
+        return lax.rem(site + k, nsite)
+
+    def dom_at(i):
+        return (i // 2) * 4 + side * 2 + i % 2
+
     def own_rows(i):
         return pl.ds(pl.multiple_of(i * cut, cut), cut)
 
@@ -149,11 +184,14 @@
         )
 
     def donor_copy(k):
-        to = dom_of(k)
-        return remote(sbuf.at[to], rbuf.at[dom], d_send.at[k], d_recv.at[ndom - k], (me, to))
+        to = site_of(k)
+        return remote(sbuf.at[to], rbuf.at[site], d_send.at[k], d_recv.at[nsite - k], (me, dom_at(to)))
 
     def donor_arrival(k):
-        return remote(sbuf.at[0], rbuf.at[dom_of(k)], d_send.at[k], d_recv.at[k], (me, dom_of(k)))
+        return remote(sbuf.at[0], rbuf.at[site_of(k)], d_send.at[k], d_recv.at[k], (me, dom_at(site_of(k))))
+
+    def partial_copy():
+        return remote(psend, precv, p_send.at[0], p_recv.at[0], (me, mate))
 
     def forward_copy(g, k):
         v0, v1 = GROUPS[g]
@@ -212,10 +250,43 @@
 
         lax.fori_loop(1, count, step, 0)
 
+    def peers(act):
+        for k in ORDER:
+            act(k)
+
+    def sites(act):
+        def step(t, carry):
+            act(nsite // 2 + (1 - 2 * lax.rem(t, 2)) * ((t + 1) // 2))
+            return carry
+
+        lax.fori_loop(0, nsite - 1, step, 0)
+
+    pairs = (
+        (x_in, x),
+        (part_in, part),
+        (block_in, block),
+        (speed_in, speed),
+        (freq_in, freq),
+        (time_weights_in, time_weights),
+        (shift_in, shift),
+        (weight_in, weight),
+        (count_in, count),
+    )
+    arriving = [pltpu.make_async_copy(a, b, loads.at[n]) for n, (a, b) in enumerate(pairs)]
+    for load in arriving:
+        load.start()
+
     barrier = pltpu.get_barrier_semaphore()
-    each(ndom, lambda k: pl.semaphore_signal(barrier, inc=1, device_id=(me, dom_of(k)), device_id_type=MESH))
-    each(ninst, lambda k: pl.semaphore_signal(barrier, inc=1, device_id=(inst_of(k), dom), device_id_type=MESH))
-
+    def greet(to):
+        pl.semaphore_signal(barrier, inc=1, device_id=to, device_id_type=MESH)
+
+    sites(lambda k: greet((me, dom_at(site_of(k)))))
+    peers(lambda k: greet((inst_of(k), dom)))
+    greet((me, mate))
+    greet((me, dom_of(jnp.where(dom % 2 == 0, ndom - 1, 1))))
+
+    for load in arriving:
+        load.wait()
     column = send_table(part, block, dom, ndom, rows, donors)
     lane = iota(column.shape, 1).astype(jnp.float32)
     chosen = jnp.concatenate(
@@ -223,19 +294,19 @@
     )
     for v in range(nv):
         out = jnp.dot(chosen, x[v], precision=HIGHEST, preferred_element_type=jnp.float32)
-        for q in range(ndom):
-            sbuf[q, v] = out[q * cap : (q + 1) * cap]
+        for i in range(nsite):
+            sbuf[i, v] = out[i * 2 * cap : (i + 1) * 2 * cap]
         hsend[0, v] = x[v, cells - 1 :, :]
         hsend[1, v] = x[v, :1, :]
 
-    pl.semaphore_wait(barrier, ndom - 1 + ninst - 1)
+    pl.semaphore_wait(barrier, nsite - 1 + ninst - 1 + 2)
     halo_copy(0).start()
     halo_copy(1).start()
-    each(ndom, lambda k: donor_copy(k).start())
+    sites(lambda k: donor_copy(k).start())
     for g in range(len(GROUPS)):
-        each(ninst, lambda k: forward_copy(g, k).start())
-
-    rbuf[dom] = sbuf[dom]
+        peers(lambda k: forward_copy(g, k).start())
+
+    rbuf[site] = sbuf[site]
     for v in range(nv):
         fbuf[0, v] = x[v, own_rows(me), :]
 
@@ -246,7 +317,9 @@
         return carry
 
     lax.fori_loop(0, ninst, weights_of, 0)
-    table = weight_table(part, weight, count, dom, ndom, rows, donors)
+    table = jnp.concatenate(
+        [weight_table(part, weight, count, whose, side, ndom, rows, donors) for whose in (dom, mate)], axis=0
+    )
 
     halo_copy(0).wait_recv()
     halo_copy(1).wait_recv()
@@ -295,16 +368,23 @@
             return carry
 
         lax.fori_loop(0, (v1 - v0) * (cut // 8), tile, 0)
-        each(ninst, lambda k: back_copy(g, k).start())
+        peers(lambda k: back_copy(g, k).start())
 
     def remap():
-        each(ndom, lambda k: donor_arrival(k).wait_recv())
+        each(nsite, lambda k: donor_arrival(k).wait_recv())
+        own = []
         for v in range(nv):
-            arrived = jnp.concatenate([rbuf[p, v] for p in range(ndom)], axis=0)
-            rows_v = jnp.dot(table, arrived, precision=HIGHEST, preferred_element_type=jnp.float32)
+            arrived = jnp.concatenate([rbuf[i, v] for i in range(nsite)], axis=0)
+            both = jnp.dot(table, arrived, precision=HIGHEST, preferred_element_type=jnp.float32)
+            own.append(both[:rows])
+            psend[v] = both[rows:]
+        partial_copy().start()
+        partial_copy().wait_recv()
+        for v in range(nv):
+            rows_v = own[v] + precv[v]
             for s in range(ninst):
                 mbuf[s, fine * v : fine * (v + 1)] = rows_v[fine * s : fine * (s + 1)]
-        each(ninst, lambda k: mapped_copy(k).start())
+        peers(lambda k: mapped_copy(k).start())
         mrec[0] = mbuf[me]
 
     def interpolate():
@@ -318,33 +398,60 @@
             return carry
 
         lax.fori_loop(0, ninst, one, 0)
-        each(ninst, lambda k: ghost_copy(k).start())
+        peers(lambda k: ghost_copy(k).start())
         gback[me] = gout[0]
 
+    mix(0)
     remap()
-    mix(0)
     mix(1)
     interpolate()
     mix(2)
 
-    for g, (v0, v1) in enumerate(GROUPS):
-        each(ninst, lambda k: back_arrival(g, k).wait_recv())
-        for v in range(v0, v1):
-            res[v] = res[v] + back[v]
+    def store(v):
+        return pltpu.make_async_copy(res.at[v], res_out.at[v], stores.at[v])
+
     each(ninst, lambda k: ghost_arrival(k).wait_recv())
     for v in range(nv):
         full = jnp.concatenate([gback[s, fine * v : fine * (v + 1)] for s in range(ninst)], axis=0)
         ghost[v] = full
         res[v, :rows] = res[v, :rows] + 0.5 * full
+    store_ghost = pltpu.make_async_copy(ghost, ghost_out, stores.at[nv])
+    store_ghost.start()
+    for g, (v0, v1) in enumerate(GROUPS):
+        each(ninst, lambda k: back_arrival(g, k).wait_recv())
+        for v in range(v0, v1):
+            res[v] = res[v] + back[v]
+            store(v).start()
 
     halo_copy(0).wait_send()
     halo_copy(1).wait_send()
-    each(ndom, lambda k: donor_copy(k).wait_send())
+    each(nsite, lambda k: donor_copy(k).wait_send())
+    partial_copy().wait_send()
     for g in range(len(GROUPS)):
         each(ninst, lambda k: forward_copy(g, k).wait_send())
         each(ninst, lambda k: back_copy(g, k).wait_send())
     each(ninst, lambda k: mapped_copy(k).wait_send())
     each(ninst, lambda k: ghost_copy(k).wait_send())
+    for v in range(nv):
+        store(v).wait()
+    store_ghost.wait()
+
+
+def place(res_in, ghost_in, res, ghost, held, held_ghost, loads, stores):
+    count = res.shape[0]
+    ways = [(res_in.at[v], held.at[v], res.at[v]) for v in range(count)]
+    ways.append((ghost_in, held_ghost, ghost))
+    moves = [
+        (pltpu.make_async_copy(a, b, loads.at[n]), pltpu.make_async_copy(b, c, stores.at[n]))
+        for n, (a, b, c) in enumerate(ways)
+    ]
+    for load, _ in moves:
+        load.start()
+    for load, store in moves:
+        load.wait()
+        store.start()
+    for _, store in moves:
+        store.wait()
 
 
 def solution(mesh):
@@ -359,8 +466,7 @@
         cut = cells // ninst
         fine = rows // ninst
         groups = len(GROUPS)
-        vmem = pl.BlockSpec(memory_space=pltpu.VMEM)
-        smem = pl.BlockSpec(memory_space=pltpu.SMEM)
+        hbm = pl.BlockSpec(memory_space=pltpu.HBM)
         f32 = jnp.float32
         dma = pltpu.SemaphoreType.DMA
         res, ghost = pl.pallas_call(
@@ -369,14 +475,29 @@
                 jax.ShapeDtypeStruct((nv, cells, pitch), f32),
                 jax.ShapeDtypeStruct((nv, rows, pitch), f32),
             ),
-            in_specs=[vmem, smem, smem, smem, smem, vmem, vmem, vmem, vmem],
-            out_specs=(vmem, vmem),
+            in_specs=[hbm] * 9,
+            out_specs=(hbm, hbm),
             scratch_shapes=[
-                pltpu.VMEM((ndom, nv, cap, pitch), f32),
-                pltpu.VMEM((ndom, nv, cap, pitch), f32),
+                pltpu.VMEM(x.shape, f32),
+                pltpu.SMEM(speed.shape, f32),
+                pltpu.SMEM(freq.shape, f32),
+                pltpu.SMEM(time_weights.shape, f32),
+                pltpu.SMEM(shift.shape, jnp.int32),
+                pltpu.VMEM(part.T.shape, jnp.int32),
+                pltpu.VMEM(part.T.shape, jnp.int32),
+                pltpu.VMEM(part.T.shape, f32),
+                pltpu.VMEM((1, count.shape[0]), jnp.int32),
+                dma((9,)),
+                pltpu.VMEM((nv, cells, pitch), f32),
+                pltpu.VMEM((nv, rows, pitch), f32),
+                dma((nv + 1,)),
+                pltpu.VMEM((ndom // 2, nv, 2 * cap, pitch), f32),
+                pltpu.VMEM((ndom // 2, nv, 2 * cap, pitch), f32),
                 pltpu.VMEM((ninst, nv, cut, pitch), f32),
                 pltpu.VMEM((ninst, nv, cut, pitch), f32),
                 pltpu.VMEM((nv, cells, pitch), f32),
+                pltpu.VMEM((nv, rows, pitch), f32),
+                pltpu.VMEM((nv, rows, pitch), f32),
                 pltpu.VMEM((ninst, nv * fine, pitch), f32),
                 pltpu.VMEM((ninst, nv * fine, pitch), f32),
                 pltpu.VMEM((ninst, nv * fine, pitch), f32),
@@ -384,12 +505,14 @@
                 pltpu.VMEM((2, nv, 1, pitch), f32),
                 pltpu.VMEM((2, nv, 1, pitch), f32),
                 pltpu.SMEM((ninst * ninst,), f32),
-                dma((ndom,)),
-                dma((ndom,)),
+                dma((ndom // 2,)),
+                dma((ndom // 2,)),
                 dma((groups, ninst)),
                 dma((groups, ninst)),
                 dma((groups, ninst)),
                 dma((groups, ninst)),
+                dma((1,)),
+                dma((1,)),
                 dma((ninst,)),
                 dma((ninst,)),
                 dma((ninst,)),
@@ -398,10 +521,27 @@
                 dma((2,)),
             ],
             compiler_params=pltpu.CompilerParams(
-                collective_id=0, has_side_effects=True, vmem_limit_bytes=40 << 20
+                collective_id=0, has_side_effects=True, vmem_limit_bytes=VMEM
             ),
             name="harmonic_residual",
         )(x, speed, freq, time_weights, shift, part.T, block.T, weight.T, count[None])
+        res, ghost = pl.pallas_call(
+            place,
+            out_shape=(
+                jax.ShapeDtypeStruct((nv, cells, pitch), f32),
+                jax.ShapeDtypeStruct((nv, rows, pitch), f32),
+            ),
+            in_specs=[hbm, hbm],
+            out_specs=(hbm, hbm),
+            scratch_shapes=[
+                pltpu.VMEM((nv, cells, pitch), f32),
+                pltpu.VMEM((nv, rows, pitch), f32),
+                dma((nv + 1,)),
+                dma((nv + 1,)),
+            ],
+            compiler_params=pltpu.CompilerParams(vmem_limit_bytes=VMEM),
+            name="place_results",
+        )(res, ghost)
         return res[None], ghost[None]
 
     in_specs = (P("inst", None, "dom", None), P(), P(), P(), P(), P(), P(), P(), P())

time: 65.8 us -> 59.5 us (0.904)
  local copies, waits for them, and re-layouts: 5.38 us -> 0 us
  Pallas kernels: 58.7 us -> 57.3 us
    unnamed x18 -> x0, local copies, waits for them, and re-layouts: 5.38 us -> none
    pallas_call x1, Pallas kernels: 58.7 us -> 55.3 us  [body(): pl.pallas_call(functools.partial(kernel, ninst, ndom), out_shape=(jax.Sha...]
    pallas_call x0 -> x1, Pallas kernels: none -> 1.95 us  [body(): pl.pallas_call(place, out_shape=(jax.ShapeDtypeStruct((nv, cells, pitch),...]
where the time goes in v2:
time: 59.5 us; the launch traced here: 58.5 us
  Pallas kernels  57.3 us (96%)
  between operations  1.29 us (2%)
    pallas_call x1, Pallas kernels, body(): pl.pallas_call(functools.partial(kernel, ninst, ndom), out_shape=(jax.Sha...  55.3 us
    pallas_call x1, Pallas kernels, body(): pl.pallas_call(place, out_shape=(jax.ShapeDtypeStruct((nv, cells, pitch),...  1.95 us

profile of v2, /device:TPU:1, one launch (start us, length us, event | category | flops | bytes accessed | tf_op | source)
XLA Modules:
  0.0 58.5 jit_solution(14185382156572436316)
XLA Ops:
  1.3 55.3 %harmonic_residual.1 = (f32[5,256,128]{2,1,0:T(8,128)}, f32[5,32,128]{2,1,0:T(8,128)}) custom-call(f32[5,256,128]{2,1,0:T(8,128)} %bitcast.7, f32[5]{0:T(128)} %speed_in.1, f32[1]{0:T(128)S(6)} %copy.11.freq_in, f32[16]{0:T(128)} %time_weights_in.1, s32[16]{0:T(128)} %shift_in.1, s32[4,1024]{1,0:T(4,128)} %bitcast.8, s32[4,1024]{1,0:T(4,128)} %bitcast.9, ...), custom_call_target="tpu_custom_call" | custom-call | tf_op jit(solution)/shard_map/harmonic_residual/pallas_call | solution.py:472
  56.6 1.9 %place_results.1 = (f32[5,256,128]{2,1,0:T(8,128)}, f32[5,32,128]{2,1,0:T(8,128)}) custom-call(f32[5,256,128]{2,1,0:T(8,128)} %get-tuple-element.6.res_in, f32[5,32,128]{2,1,0:T(8,128)} %get-tuple-element.7.ghost_in), custom_call_target="tpu_custom_call" | custom-call | tf_op jit(solution)/shard_map/place_results/pallas_call | solution.py:528

commit v3 on v2

--- a/solution.py
+++ b/solution.py
@@ -9,9 +9,9 @@
 from jax.sharding import PartitionSpec as P
 
 HIGHEST = lax.Precision.HIGHEST
-VMEM = 56 << 20
+VMEM = 32 << 20
 MESH = pl.DeviceIdType.MESH
-GROUPS = ((0, 2), (2, 4), (4, 5))
+GROUPS = ((0, 5),)
 ORDER = (2, 10, 6, 14, 9, 5, 11, 7, 1, 13, 3, 15, 8, 4, 12)
 
 
@@ -106,8 +106,8 @@
     block_in,
     weight_in,
     count_in,
-    res_out,
-    ghost_out,
+    res,
+    ghost,
     x,
     speed,
     freq,
@@ -118,9 +118,6 @@
     weight,
     count,
     loads,
-    res,
-    ghost,
-    stores,
     sbuf,
     rbuf,
     fbuf,
@@ -135,6 +132,7 @@
     hsend,
     hrecv,
     wtab,
+    go,
     d_send,
     d_recv,
     f_send,
@@ -168,6 +166,12 @@
     side = (dom // 2) % 2
     site = (dom // 4) * 2 + dom % 2
     mate = dom + 2 - 4 * side
+    core = dom % 2
+    depth = ndom // 4
+    layer = dom // 4
+
+    def second_core_at(z, s):
+        return (me, lax.rem(z + depth, depth) * 4 + s * 2 + 1)
 
     def site_of(k):
         return lax.rem(site + k, nsite)
@@ -277,13 +281,16 @@
         load.start()
 
     barrier = pltpu.get_barrier_semaphore()
+
     def greet(to):
         pl.semaphore_signal(barrier, inc=1, device_id=to, device_id_type=MESH)
 
-    sites(lambda k: greet((me, dom_at(site_of(k)))))
-    peers(lambda k: greet((inst_of(k), dom)))
-    greet((me, mate))
-    greet((me, dom_of(jnp.where(dom % 2 == 0, ndom - 1, 1))))
+    peers(lambda k: greet((inst_of(k), dom - core)))
+    greet((me, dom + 1 - 2 * core))
+    for k in range(1, depth):
+        greet(second_core_at(layer + k, side))
+    greet(second_core_at(layer, 1 - side))
+    greet(second_core_at(layer - 1 + 2 * side, 1 - side))
 
     for load in arriving:
         load.wait()
@@ -299,12 +306,30 @@
         hsend[0, v] = x[v, cells - 1 :, :]
         hsend[1, v] = x[v, :1, :]
 
-    pl.semaphore_wait(barrier, nsite - 1 + ninst - 1 + 2)
+    @pl.when(core == 0)
+    def _():
+        pl.semaphore_wait(barrier, 2 * (ninst - 1) + 1)
+        pl.semaphore_signal(go.at[0], inc=1, device_id=(me, dom + 1), device_id_type=MESH)
+
+    @pl.when(core == 1)
+    def _():
+        pl.semaphore_wait(go.at[0], 1)
+
+    for g in range(len(GROUPS)):
+        peers(lambda k: forward_copy(g, k).start())
+
+    @pl.when(core == 1)
+    def _():
+        pl.semaphore_wait(barrier, 2 * (depth - 1) + 2 + 2 + 1)
+        pl.semaphore_signal(go.at[1], inc=1, device_id=(me, dom - 1), device_id_type=MESH)
+
+    @pl.when(core == 0)
+    def _():
+        pl.semaphore_wait(go.at[1], 1)
+
+    sites(lambda k: donor_copy(k).start())
     halo_copy(0).start()
     halo_copy(1).start()
-    sites(lambda k: donor_copy(k).start())
-    for g in range(len(GROUPS)):
-        peers(lambda k: forward_copy(g, k).start())
 
     rbuf[site] = sbuf[site]
     for v in range(nv):
@@ -321,15 +346,11 @@
         [weight_table(part, weight, count, whose, side, ndom, rows, donors) for whose in (dom, mate)], axis=0
     )
 
-    halo_copy(0).wait_recv()
-    halo_copy(1).wait_recv()
     edge = iota((cells, pitch), 0)
     for v in range(nv):
         u = x[v]
-        low = jnp.where(dom == 0, 0.0, hrecv[0, v])
-        high = jnp.where(dom == ndom - 1, 0.0, hrecv[1, v])
-        below = jnp.where(edge == 0, low, pltpu.roll(u, 1, 0))
-        above = jnp.where(edge == cells - 1, high, pltpu.roll(u, cells - 1, 0))
+        below = jnp.where(edge == 0, 0.0, pltpu.roll(u, 1, 0))
+        above = jnp.where(edge == cells - 1, 0.0, pltpu.roll(u, cells - 1, 0))
         upper = pltpu.roll(u, pitch - 1, 1)
         lower = pltpu.roll(u, 1, 1)
         base = 0.25 * (above + below + upper + lower - 4.0 * u) - speed[v] * (upper - lower) * 0.5
@@ -401,27 +422,24 @@
         peers(lambda k: ghost_copy(k).start())
         gback[me] = gout[0]
 
+    remap()
     mix(0)
-    remap()
-    mix(1)
     interpolate()
-    mix(2)
-
-    def store(v):
-        return pltpu.make_async_copy(res.at[v], res_out.at[v], stores.at[v])
-
+
+    halo_copy(0).wait_recv()
+    halo_copy(1).wait_recv()
+    for v in range(nv):
+        res[v, :1] = res[v, :1] + jnp.where(dom == 0, 0.0, 0.25 * hrecv[0, v])
+        res[v, cells - 1 :] = res[v, cells - 1 :] + jnp.where(dom == ndom - 1, 0.0, 0.25 * hrecv[1, v])
     each(ninst, lambda k: ghost_arrival(k).wait_recv())
     for v in range(nv):
         full = jnp.concatenate([gback[s, fine * v : fine * (v + 1)] for s in range(ninst)], axis=0)
         ghost[v] = full
         res[v, :rows] = res[v, :rows] + 0.5 * full
-    store_ghost = pltpu.make_async_copy(ghost, ghost_out, stores.at[nv])
-    store_ghost.start()
     for g, (v0, v1) in enumerate(GROUPS):
         each(ninst, lambda k: back_arrival(g, k).wait_recv())
         for v in range(v0, v1):
             res[v] = res[v] + back[v]
-            store(v).start()
 
     halo_copy(0).wait_send()
     halo_copy(1).wait_send()
@@ -432,26 +450,17 @@
         each(ninst, lambda k: back_copy(g, k).wait_send())
     each(ninst, lambda k: mapped_copy(k).wait_send())
     each(ninst, lambda k: ghost_copy(k).wait_send())
-    for v in range(nv):
-        store(v).wait()
-    store_ghost.wait()
-
-
-def place(res_in, ghost_in, res, ghost, held, held_ghost, loads, stores):
-    count = res.shape[0]
-    ways = [(res_in.at[v], held.at[v], res.at[v]) for v in range(count)]
-    ways.append((ghost_in, held_ghost, ghost))
+
+
+def place(res_in, ghost_in, res, ghost, sems):
     moves = [
-        (pltpu.make_async_copy(a, b, loads.at[n]), pltpu.make_async_copy(b, c, stores.at[n]))
-        for n, (a, b, c) in enumerate(ways)
+        pltpu.make_async_copy(res_in, res, sems.at[0]),
+        pltpu.make_async_copy(ghost_in, ghost, sems.at[1]),
     ]
-    for load, _ in moves:
-        load.start()
-    for load, store in moves:
-        load.wait()
-        store.start()
-    for _, store in moves:
-        store.wait()
+    for move in moves:
+        move.start()
+    for move in moves:
+        move.wait()
 
 
 def solution(mesh):
@@ -467,16 +476,16 @@
         fine = rows // ninst
         groups = len(GROUPS)
         hbm = pl.BlockSpec(memory_space=pltpu.HBM)
+        vmem = pl.BlockSpec(memory_space=pltpu.VMEM)
         f32 = jnp.float32
         dma = pltpu.SemaphoreType.DMA
+        given = (x, speed, freq, time_weights, shift, part.T, block.T, weight.T, count[None])
+        given = [a if a.size == 1 else pltpu.with_memory_space_constraint(a, pltpu.HBM) for a in given]
         res, ghost = pl.pallas_call(
             functools.partial(kernel, ninst, ndom),
-            out_shape=(
-                jax.ShapeDtypeStruct((nv, cells, pitch), f32),
-                jax.ShapeDtypeStruct((nv, rows, pitch), f32),
-            ),
+            out_shape=(pltpu.VMEM((nv, cells, pitch), f32), pltpu.VMEM((nv, rows, pitch), f32)),
             in_specs=[hbm] * 9,
-            out_specs=(hbm, hbm),
+            out_specs=(vmem, vmem),
             scratch_shapes=[
                 pltpu.VMEM(x.shape, f32),
                 pltpu.SMEM(speed.shape, f32),
@@ -488,9 +497,6 @@
                 pltpu.VMEM(part.T.shape, f32),
                 pltpu.VMEM((1, count.shape[0]), jnp.int32),
                 dma((9,)),
-                pltpu.VMEM((nv, cells, pitch), f32),
-                pltpu.VMEM((nv, rows, pitch), f32),
-                dma((nv + 1,)),
                 pltpu.VMEM((ndom // 2, nv, 2 * cap, pitch), f32),
                 pltpu.VMEM((ndom // 2, nv, 2 * cap, pitch), f32),
                 pltpu.VMEM((ninst, nv, cut, pitch), f32),
@@ -505,6 +511,7 @@
                 pltpu.VMEM((2, nv, 1, pitch), f32),
                 pltpu.VMEM((2, nv, 1, pitch), f32),
                 pltpu.SMEM((ninst * ninst,), f32),
+                pltpu.SemaphoreType.REGULAR((2,)),
                 dma((ndom // 2,)),
                 dma((ndom // 2,)),
                 dma((groups, ninst)),
@@ -524,24 +531,18 @@
                 collective_id=0, has_side_effects=True, vmem_limit_bytes=VMEM
             ),
             name="harmonic_residual",
-        )(x, speed, freq, time_weights, shift, part.T, block.T, weight.T, count[None])
+        )(*given)
         res, ghost = pl.pallas_call(
             place,
             out_shape=(
                 jax.ShapeDtypeStruct((nv, cells, pitch), f32),
                 jax.ShapeDtypeStruct((nv, rows, pitch), f32),
             ),
-            in_specs=[hbm, hbm],
+            in_specs=[vmem, vmem],
             out_specs=(hbm, hbm),
-            scratch_shapes=[
-                pltpu.VMEM((nv, cells, pitch), f32),
-                pltpu.VMEM((nv, rows, pitch), f32),
-                dma((nv + 1,)),
-                dma((nv + 1,)),
-            ],
-            compiler_params=pltpu.CompilerParams(vmem_limit_bytes=VMEM),
+            scratch_shapes=[dma((2,))],
             name="place_results",
-        )(res, ghost)
+        )(*(pltpu.with_memory_space_constraint(a, pltpu.VMEM) for a in (res, ghost)))
         return res[None], ghost[None]
 
     in_specs = (P("inst", None, "dom", None), P(), P(), P(), P(), P(), P(), P(), P())

time: 59.5 us -> 54.9 us (0.923); the launches traced: 58.5 us -> 54.8 us
  Pallas kernels: 57.3 us -> 53.5 us
    pallas_call x1, Pallas kernels: 55.3 us -> 52.6 us  [body(): pl.pallas_call(functools.partial(kernel, ninst, ndom), out_shape=(pltpu.V...]
    pallas_call x1, Pallas kernels: 1.95 us -> 0.87 us  [body(): pl.pallas_call(place, out_shape=(jax.ShapeDtypeStruct((nv, cells, pitch),...]
where the time goes in v3:
time: 54.9 us; the launch traced here: 54.8 us
  Pallas kernels  53.5 us (97%)
  between operations  1.29 us (2%)
    pallas_call x1, Pallas kernels, body(): pl.pallas_call(functools.partial(kernel, ninst, ndom), out_shape=(pltpu.V...  52.6 us

profile of v3, /device:TPU:1, one launch (start us, length us, event | category | flops | bytes accessed | tf_op | source)
XLA Modules:
  0.0 54.8 jit_solution(11943016920433003180)
XLA Ops:
  1.3 52.6 %harmonic_residual.1 = (f32[5,256,128]{2,1,0:T(8,128)S(1)}, f32[5,32,128]{2,1,0:T(8,128)S(1)}) custom-call(f32[5,256,128]{2,1,0:T(8,128)} %bitcast.7, f32[5]{0:T(128)} %speed_in.1, f32[1]{0:T(128)S(6)} %copy.11.freq_in, f32[16]{0:T(128)} %time_weights_in.1, s32[16]{0:T(128)} %shift_in.1, s32[4,1024]{1,0:T(4,128)} %bitcast.8, s32[4,1024]{1,0:T(4,128)} %bitcast.9, ...), custom_call_target="tpu_custom_call" | custom-call | tf_op jit(solution)/shard_map/harmonic_residual/pallas_call | solution.py:484
  53.9 0.9 %place_results.1 = (f32[5,256,128]{2,1,0:T(8,128)}, f32[5,32,128]{2,1,0:T(8,128)}) custom-call(f32[5,256,128]{2,1,0:T(8,128)S(1)} %get-tuple-element.6.res_in, f32[5,32,128]{2,1,0:T(8,128)S(1)} %get-tuple-element.7.ghost_in), custom_call_target="tpu_custom_call" | custom-call | tf_op jit(solution)/shard_map/place_results/pallas_call | solution.py:535

commit v4 on v3

--- a/solution.py
+++ b/solution.py
@@ -12,7 +12,7 @@
 VMEM = 32 << 20
 MESH = pl.DeviceIdType.MESH
 GROUPS = ((0, 5),)
-ORDER = (2, 10, 6, 14, 9, 5, 11, 7, 1, 13, 3, 15, 8, 4, 12)
+ORDER = (12, 4, 8, 15, 3, 13, 1, 7, 11, 5, 9, 14, 6, 10, 2)
 
 
 def spectral_line(length):
@@ -123,8 +123,6 @@
     fbuf,
     obuf,
     back,
-    psend,
-    precv,
     mbuf,
     mrec,
     gout,
@@ -139,8 +137,6 @@
     f_recv,
     b_send,
     b_recv,
-    p_send,
-    p_recv,
     m_send,
     m_recv,
     g_send,
@@ -170,8 +166,8 @@
     depth = ndom // 4
     layer = dom // 4
 
-    def second_core_at(z, s):
-        return (me, lax.rem(z + depth, depth) * 4 + s * 2 + 1)
+    def first_core_at(z, s):
+        return lax.rem(z + depth, depth) * 4 + s * 2
 
     def site_of(k):
         return lax.rem(site + k, nsite)
@@ -193,9 +189,6 @@
 
     def donor_arrival(k):
         return remote(sbuf.at[0], rbuf.at[site_of(k)], d_send.at[k], d_recv.at[k], (me, dom_at(site_of(k))))
-
-    def partial_copy():
-        return remote(psend, precv, p_send.at[0], p_recv.at[0], (me, mate))
 
     def forward_copy(g, k):
         v0, v1 = GROUPS[g]
@@ -230,12 +223,16 @@
             obuf.at[k, v0:v1], back.at[v0:v1, own_rows(inst_of(k))], b_send.at[g, k], b_recv.at[g, k], (inst_of(k), dom)
         )
 
-    def mapped_copy(k):
-        to = inst_of(k)
-        return remote(mbuf.at[to], mrec.at[ninst - k], m_send.at[k], m_recv.at[ninst - k], (to, dom))
-
-    def mapped_arrival(k):
-        return remote(mbuf.at[0], mrec.at[k], m_send.at[k], m_recv.at[k], (inst_of(k), dom))
+    def mapped_copy(n, k):
+        to, slot = inst_of(k), (ninst - k) % ninst
+        return remote(
+            mbuf.at[n, to], mrec.at[n, slot], m_send.at[n, k], m_recv.at[n, slot], (to, mate if n else dom)
+        )
+
+    def mapped_arrival(n, k):
+        return remote(
+            mbuf.at[n, 0], mrec.at[n, k], m_send.at[n, k], m_recv.at[n, k], (inst_of(k), mate if n else dom)
+        )
 
     def ghost_copy(k):
         return remote(gout.at[k], gback.at[me], g_send.at[k], g_recv.at[ninst - k], (inst_of(k), dom))
@@ -264,6 +261,23 @@
             return carry
 
         lax.fori_loop(0, nsite - 1, step, 0)
+
+    barrier = pltpu.get_barrier_semaphore()
+
+    def greet(to):
+        pl.semaphore_signal(barrier, inc=1, device_id=to, device_id_type=MESH)
+
+    peers(lambda k: greet((inst_of(k), dom)))
+
+    @pl.when(core == 1)
+    def _():
+        greet((me, dom - 1))
+
+    for k in range(1, depth):
+        greet((me, first_core_at(layer + k, side)))
+    greet((me, first_core_at(layer - 1 + 2 * side, 1 - side)))
+    for k in (0, *ORDER):
+        greet((inst_of(k), first_core_at(layer, 1 - side)))
 
     pairs = (
         (x_in, x),
@@ -280,18 +294,6 @@
     for load in arriving:
         load.start()
 
-    barrier = pltpu.get_barrier_semaphore()
-
-    def greet(to):
-        pl.semaphore_signal(barrier, inc=1, device_id=to, device_id_type=MESH)
-
-    peers(lambda k: greet((inst_of(k), dom - core)))
-    greet((me, dom + 1 - 2 * core))
-    for k in range(1, depth):
-        greet(second_core_at(layer + k, side))
-    greet(second_core_at(layer, 1 - side))
-    greet(second_core_at(layer - 1 + 2 * side, 1 - side))
-
     for load in arriving:
         load.wait()
     column = send_table(part, block, dom, ndom, rows, donors)
@@ -306,26 +308,21 @@
         hsend[0, v] = x[v, cells - 1 :, :]
         hsend[1, v] = x[v, :1, :]
 
+    @pl.when(core == 1)
+    def _():
+        pl.semaphore_wait(barrier, ninst - 1)
+
     @pl.when(core == 0)
     def _():
-        pl.semaphore_wait(barrier, 2 * (ninst - 1) + 1)
+        pl.semaphore_wait(barrier, ninst - 1 + 1 + 2 * (depth - 1) + 2 + 2 * ninst)
         pl.semaphore_signal(go.at[0], inc=1, device_id=(me, dom + 1), device_id_type=MESH)
+
+    for g in range(len(GROUPS)):
+        peers(lambda k: forward_copy(g, k).start())
 
     @pl.when(core == 1)
     def _():
         pl.semaphore_wait(go.at[0], 1)
-
-    for g in range(len(GROUPS)):
-        peers(lambda k: forward_copy(g, k).start())
-
-    @pl.when(core == 1)
-    def _():
-        pl.semaphore_wait(barrier, 2 * (depth - 1) + 2 + 2 + 1)
-        pl.semaphore_signal(go.at[1], inc=1, device_id=(me, dom - 1), device_id_type=MESH)
-
-    @pl.when(core == 0)
-    def _():
-        pl.semaphore_wait(go.at[1], 1)
 
     sites(lambda k: donor_copy(k).start())
     halo_copy(0).start()
@@ -393,28 +390,28 @@
 
     def remap():
         each(nsite, lambda k: donor_arrival(k).wait_recv())
-        own = []
         for v in range(nv):
             arrived = jnp.concatenate([rbuf[i, v] for i in range(nsite)], axis=0)
             both = jnp.dot(table, arrived, precision=HIGHEST, preferred_element_type=jnp.float32)
-            own.append(both[:rows])
-            psend[v] = both[rows:]
-        partial_copy().start()
-        partial_copy().wait_recv()
-        for v in range(nv):
-            rows_v = own[v] + precv[v]
-            for s in range(ninst):
-                mbuf[s, fine * v : fine * (v + 1)] = rows_v[fine * s : fine * (s + 1)]
-        peers(lambda k: mapped_copy(k).start())
-        mrec[0] = mbuf[me]
+            for n in range(2):
+                for s in range(ninst):
+                    at = n * rows + fine * s
+                    mbuf[n, s, fine * v : fine * (v + 1)] = both[at : at + fine]
+        peers(lambda k: mapped_copy(0, k).start())
+        mapped_copy(1, 0).start()
+        peers(lambda k: mapped_copy(1, k).start())
+        mrec[0, 0] = mbuf[0, me]
 
     def interpolate():
-        each(ninst, lambda k: mapped_arrival(k).wait_recv())
+        each(ninst, lambda k: mapped_arrival(0, k).wait_recv())
+        mapped_arrival(1, 0).wait_recv()
+        each(ninst, lambda k: mapped_arrival(1, k).wait_recv())
+        mrec[0] = mrec[0] + mrec[1]
 
         def one(target, carry):
-            total = wtab[target * ninst] * mrec[0]
+            total = wtab[target * ninst] * mrec[0, 0]
             for k in range(1, ninst):
-                total = total + wtab[target * ninst + k] * mrec[k]
+                total = total + wtab[target * ninst + k] * mrec[0, k]
             gout[target] = total
             return carry
 
@@ -431,24 +428,25 @@
     for v in range(nv):
         res[v, :1] = res[v, :1] + jnp.where(dom == 0, 0.0, 0.25 * hrecv[0, v])
         res[v, cells - 1 :] = res[v, cells - 1 :] + jnp.where(dom == ndom - 1, 0.0, 0.25 * hrecv[1, v])
+    for g, (v0, v1) in enumerate(GROUPS):
+        each(ninst, lambda k: back_arrival(g, k).wait_recv())
+        for v in range(v0, v1):
+            res[v] = res[v] + back[v]
     each(ninst, lambda k: ghost_arrival(k).wait_recv())
     for v in range(nv):
         full = jnp.concatenate([gback[s, fine * v : fine * (v + 1)] for s in range(ninst)], axis=0)
         ghost[v] = full
         res[v, :rows] = res[v, :rows] + 0.5 * full
-    for g, (v0, v1) in enumerate(GROUPS):
-        each(ninst, lambda k: back_arrival(g, k).wait_recv())
-        for v in range(v0, v1):
-            res[v] = res[v] + back[v]
 
     halo_copy(0).wait_send()
     halo_copy(1).wait_send()
     each(nsite, lambda k: donor_copy(k).wait_send())
-    partial_copy().wait_send()
     for g in range(len(GROUPS)):
         each(ninst, lambda k: forward_copy(g, k).wait_send())
         each(ninst, lambda k: back_copy(g, k).wait_send())
-    each(ninst, lambda k: mapped_copy(k).wait_send())
+    each(ninst, lambda k: mapped_copy(0, k).wait_send())
+    mapped_copy(1, 0).wait_send()
+    each(ninst, lambda k: mapped_copy(1, k).wait_send())
     each(ninst, lambda k: ghost_copy(k).wait_send())
 
 
@@ -502,26 +500,22 @@
                 pltpu.VMEM((ninst, nv, cut, pitch), f32),
                 pltpu.VMEM((ninst, nv, cut, pitch), f32),
                 pltpu.VMEM((nv, cells, pitch), f32),
-                pltpu.VMEM((nv, rows, pitch), f32),
-                pltpu.VMEM((nv, rows, pitch), f32),
-                pltpu.VMEM((ninst, nv * fine, pitch), f32),
-                pltpu.VMEM((ninst, nv * fine, pitch), f32),
+                pltpu.VMEM((2, ninst, nv * fine, pitch), f32),
+                pltpu.VMEM((2, ninst, nv * fine, pitch), f32),
                 pltpu.VMEM((ninst, nv * fine, pitch), f32),
                 pltpu.VMEM((ninst, nv * fine, pitch), f32),
                 pltpu.VMEM((2, nv, 1, pitch), f32),
                 pltpu.VMEM((2, nv, 1, pitch), f32),
                 pltpu.SMEM((ninst * ninst,), f32),
-                pltpu.SemaphoreType.REGULAR((2,)),
+                pltpu.SemaphoreType.REGULAR((1,)),
                 dma((ndom // 2,)),
                 dma((ndom // 2,)),
                 dma((groups, ninst)),
                 dma((groups, ninst)),
                 dma((groups, ninst)),
                 dma((groups, ninst)),
-                dma((1,)),
-                dma((1,)),
-                dma((ninst,)),
-                dma((ninst,)),
+                dma((2, ninst)),
+                dma((2, ninst)),
                 dma((ninst,)),
                 dma((ninst,)),
                 dma((2,)),

time: 54.9 us -> 53.3 us (0.971)
  Pallas kernels: 53.5 us -> 51.5 us
    pallas_call x1, Pallas kernels: 52.6 us -> 50.7 us  [body(): pl.pallas_call(functools.partial(kernel, ninst, ndom), out_shape=(pltpu.V...]
where the time goes in v4:
time: 53.3 us; the launch traced here: 52.8 us
  Pallas kernels  51.5 us (97%)
  between operations  1.29 us (2%)
    pallas_call x1, Pallas kernels, body(): pl.pallas_call(functools.partial(kernel, ninst, ndom), out_shape=(pltpu.V...  50.7 us

profile of v4, /device:TPU:1, one launch (start us, length us, event | category | flops | bytes accessed | tf_op | source)
XLA Modules:
  0.0 52.8 jit_solution(17925018373866921710)
XLA Ops:
  1.3 50.7 %harmonic_residual.1 = (f32[5,256,128]{2,1,0:T(8,128)S(1)}, f32[5,32,128]{2,1,0:T(8,128)S(1)}) custom-call(f32[5,256,128]{2,1,0:T(8,128)} %bitcast.7, f32[5]{0:T(128)} %speed_in.1, f32[1]{0:T(128)S(6)} %copy.11.freq_in, f32[16]{0:T(128)} %time_weights_in.1, s32[16]{0:T(128)} %shift_in.1, s32[4,1024]{1,0:T(4,128)} %bitcast.8, s32[4,1024]{1,0:T(4,128)} %bitcast.9, ...), custom_call_target="tpu_custom_call" | custom-call | tf_op jit(solution)/shard_map/harmonic_residual/pallas_call | solution.py:482
  51.9 0.9 %place_results.1 = (f32[5,256,128]{2,1,0:T(8,128)}, f32[5,32,128]{2,1,0:T(8,128)}) custom-call(f32[5,256,128]{2,1,0:T(8,128)S(1)} %get-tuple-element.6.res_in, f32[5,32,128]{2,1,0:T(8,128)S(1)} %get-tuple-element.7.ghost_in), custom_call_target="tpu_custom_call" | custom-call | tf_op jit(solution)/shard_map/place_results/pallas_call | solution.py:529

commit v5 on v4

--- a/solution.py
+++ b/solution.py
@@ -255,6 +255,10 @@
         for k in ORDER:
             act(k)
 
+    def far_peers(act):
+        for k in reversed(ORDER):
+            act(k)
+
     def sites(act):
         def step(t, carry):
             act(nsite // 2 + (1 - 2 * lax.rem(t, 2)) * ((t + 1) // 2))
@@ -317,14 +321,21 @@
         pl.semaphore_wait(barrier, ninst - 1 + 1 + 2 * (depth - 1) + 2 + 2 * ninst)
         pl.semaphore_signal(go.at[0], inc=1, device_id=(me, dom + 1), device_id_type=MESH)
 
-    for g in range(len(GROUPS)):
-        peers(lambda k: forward_copy(g, k).start())
+    def forward():
+        for g in range(len(GROUPS)):
+            peers(lambda k: forward_copy(g, k).start())
+
+    @pl.when(core == 0)
+    def _():
+        sites(lambda k: donor_copy(k).start())
+        forward()
 
     @pl.when(core == 1)
     def _():
+        forward()
         pl.semaphore_wait(go.at[0], 1)
-
-    sites(lambda k: donor_copy(k).start())
+        sites(lambda k: donor_copy(k).start())
+
     halo_copy(0).start()
     halo_copy(1).start()
 
@@ -397,9 +408,9 @@
                 for s in range(ninst):
                     at = n * rows + fine * s
                     mbuf[n, s, fine * v : fine * (v + 1)] = both[at : at + fine]
-        peers(lambda k: mapped_copy(0, k).start())
+        far_peers(lambda k: mapped_copy(0, k).start())
         mapped_copy(1, 0).start()
-        peers(lambda k: mapped_copy(1, k).start())
+        far_peers(lambda k: mapped_copy(1, k).start())
         mrec[0, 0] = mbuf[0, me]
 
     def interpolate():
@@ -416,7 +427,7 @@
             return carry
 
         lax.fori_loop(0, ninst, one, 0)
-        peers(lambda k: ghost_copy(k).start())
+        far_peers(lambda k: ghost_copy(k).start())
         gback[me] = gout[0]
 
     remap()

time: 53.3 us -> 53.1 us (level)
  no operation moved by 1% of the time
where the time goes in v5:
time: 53.1 us; the launch traced here: 53 us
  Pallas kernels  51.7 us (97%)
  between operations  1.29 us (2%)
    pallas_call x1, Pallas kernels, body(): pl.pallas_call(functools.partial(kernel, ninst, ndom), out_shape=(pltpu.V...  50.8 us

profile of v5, /device:TPU:1, one launch (start us, length us, event | category | flops | bytes accessed | tf_op | source)
XLA Modules:
  0.0 53.0 jit_solution(1667267584450971525)
XLA Ops:
  1.3 50.8 %harmonic_residual.1 = (f32[5,256,128]{2,1,0:T(8,128)S(1)}, f32[5,32,128]{2,1,0:T(8,128)S(1)}) custom-call(f32[5,256,128]{2,1,0:T(8,128)} %bitcast.7, f32[5]{0:T(128)} %speed_in.1, f32[1]{0:T(128)S(6)} %copy.11.freq_in, f32[16]{0:T(128)} %time_weights_in.1, s32[16]{0:T(128)} %shift_in.1, s32[4,1024]{1,0:T(4,128)} %bitcast.8, s32[4,1024]{1,0:T(4,128)} %bitcast.9, ...), custom_call_target="tpu_custom_call" | custom-call | tf_op jit(solution)/shard_map/harmonic_residual/pallas_call | solution.py:493
  52.1 0.9 %place_results.1 = (f32[5,256,128]{2,1,0:T(8,128)}, f32[5,32,128]{2,1,0:T(8,128)}) custom-call(f32[5,256,128]{2,1,0:T(8,128)S(1)} %get-tuple-element.6.res_in, f32[5,32,128]{2,1,0:T(8,128)S(1)} %get-tuple-element.7.ghost_in), custom_call_target="tpu_custom_call" | custom-call | tf_op jit(solution)/shard_map/place_results/pallas_call | solution.py:540
